TPU v7x, 256 devices: a whole 4x4x8 slice. The times are simulated.
256 devices in a mesh: gx: 16 (over y, x), yz: 16 (over z, core).
Axes of the slice: x: 4, y: 4, z: 8, core: 2. Of those that a mesh axis runs over, the one named last changes fastest.
Arguments:
- tokens: bfloat16 [512, 9216], P(None, ('gx', 'yz')), may hold values from -6 to 6
- gate_weight: bfloat16 [9216, 36864], P('gx', 'yz'), may hold values from -0.0625 to 0.0625
- up_weight: bfloat16 [9216, 36864], P('gx', 'yz'), may hold values from -0.0625 to 0.0625
- down_weight: bfloat16 [36864, 9216], P('yz', 'gx'), may hold values from -0.03125 to 0.03125
- exponents_hidden: int32 [16, 576], P('gx', 'yz'), may hold values from -9 to -6
- exponents_output: int32 [16, 144], P('yz', 'gx'), may hold values from -9 to -6
Outputs:
- mixed: bfloat16 [512, 9216], P(None, ('gx', 'yz'))
- hidden: bfloat16 [512, 36864], P(None, ('yz', 'gx'))
All inputs are finite; a program needn't handle non-finite values.
Results may differ from a plain program's by a relative error of at most 0.034.
Values may be sent and summed in bfloat16 or wider, within the bound.
A program may use at most 64 MiB of HBM per device.

v0:
```python
import jax
import jax.numpy as jnp
from jax import lax
from jax.sharding import PartitionSpec as P

saturation = 127.0


def saturate(partial_value, exponents):
    scale = jnp.repeat(
        jnp.exp2(exponents.astype(jnp.float32)), partial_value.shape[-1] // exponents.shape[-1]
    )
    return jnp.clip(partial_value / scale, -saturation, saturation) * scale


def on_device(tokens, gate_weight, up_weight, down_weight, exponents_hidden, exponents_output):
    piece = lax.all_gather(tokens, "yz", axis=1, tiled=True)
    gate_part = jnp.dot(piece, gate_weight, preferred_element_type=jnp.float32)
    up_part = jnp.dot(piece, up_weight, preferred_element_type=jnp.float32)
    gate_term = saturate(gate_part, exponents_hidden[0])
    up_term = saturate(up_part, exponents_hidden[0])
    gate_sum, up_sum = (
        lax.psum_scatter(
            gate_term.astype(jnp.bfloat16), "gx", scatter_dimension=1, tiled=True
        ).astype(jnp.float32),
        lax.psum_scatter(
            up_term.astype(jnp.bfloat16), "gx", scatter_dimension=1, tiled=True
        ).astype(jnp.float32),
    )
    hidden = (jax.nn.silu(gate_sum) * up_sum).astype(jnp.bfloat16)
    output_part = jnp.dot(
        lax.all_gather(hidden, "gx", axis=1, tiled=True),
        down_weight,
        preferred_element_type=jnp.float32,
    )
    output_term = saturate(output_part, exponents_output[0])
    mixed = lax.psum_scatter(
        output_term.astype(jnp.bfloat16), "yz", scatter_dimension=1, tiled=True
    )
    return (mixed, hidden)


def solution(mesh):
    placed = (
        P(None, ("gx", "yz")),
        P("gx", "yz"),
        P("gx", "yz"),
        P("yz", "gx"),
        P("gx", "yz"),
        P("yz", "gx"),
    )
    return jax.shard_map(
        on_device,
        mesh=mesh,
        in_specs=placed,
        out_specs=(P(None, ("gx", "yz")), P(None, ("yz", "gx"))),
        check_vma=False,
    )
```

profile of v0, /device:TPU:1, one launch (start us, length us, event | category | flops | bytes accessed | tf_op | source)
XLA Modules:
  0.0 295.8 jit_solution(7855707909450580168)
XLA Ops:
  7.2 0.0 copy-start
  7.2 0.0 reduce-scatter.5.cloned.1.call-start
  7.2 23.5 %all-gather = bf16[16,36,512]{2,1,0:T(8,128)(2,1)S(1)} all-gather(bf16[1,36,512]{2,1,0:T(8,128)(2,1)} %bitcast.16), channel_id=1, replica_groups=mesh['gx'=16,'yz'=16] {'yz'}, dimensions={0}, use_global_device_ids=true | all-gather | bytes 626688 | tf_op jit(solution)/shard_map/all_gather | solution.py:17
  30.7 0.9 reshape.15
  31.7 0.7 exponential_bitcast_fusion.1
  32.3 0.1 broadcast_in_dim.7
  32.4 0.1 div.30
  32.5 0.0 copy-done
  32.5 0.0 copy-start.1
  32.5 4.7 %multiply_convert_fusion.1 = bf16[512,2304]{0,1:T(8,128)(2,1)} fusion(bf16[576,512]{1,0:T(8,128)(2,1)} %reshape.15, bf16[576,2304]{1,0:T(8,128)(2,1)S(1)} %copy-done, f32[2304]{0:T(1024)S(1)} %div.30), kind=kOutput, calls=%fused_computation.1 | convolution fusion | flops 1363673088 | bytes 5612544 | tf_op jit(solution)/shard_map/dot_general | solution.py:18
  37.2 0.0 reduce-scatter.5.cloned.1.call-update
  37.2 0.0 reduce-scatter.7.cloned.1.call-start
  37.3 0.0 copy-done.1
  37.3 5.4 %multiply_convert_fusion = bf16[512,2304]{0,1:T(8,128)(2,1)} fusion(bf16[576,512]{1,0:T(8,128)(2,1)S(1)} %copy-done.1, bf16[576,2304]{1,0:T(8,128)(2,1)} %param.8, f32[2304]{0:T(1024)S(1)} %div.30), kind=kOutput, calls=%fused_computation | convolution fusion | flops 1363673088 | bytes 5612544 | tf_op jit(solution)/shard_map/dot_general | solution.py:19
  42.7 0.0 copy-start.3
  42.7 0.0 reduce-scatter.7.cloned.1.call-update
  42.7 0.0 all-gather.3.cloned.1.call-start
  42.7 70.4 %reduce-scatter.5.cloned.1.call-done = bf16[512,144]{0,1:T(8,128)(2,1)} async-done(((bf16[512,2304]{0,1:T(8,128)(2,1)}), bf16[512,144]{0,1:T(8,128)(2,1)}) %reduce-scatter.5.cloned.1.call-update) | async-done | bytes 147472 | tf_op jit(solution)/shard_map/reduce_scatter | solution.py:23
  113.2 82.9 %reduce-scatter.7.cloned.1.call-done = bf16[512,144]{0,1:T(8,128)(2,1)} async-done(((bf16[512,2304]{0,1:T(8,128)(2,1)}), bf16[512,144]{0,1:T(8,128)(2,1)}) %reduce-scatter.7.cloned.1.call-update) | async-done | bytes 147472 | tf_op jit(solution)/shard_map/reduce_scatter | solution.py:26
  196.0 1.7 fusion.8
  197.8 0.0 all-gather.3.cloned.1.call-update
  197.8 0.0 copy-done.3
  197.8 0.1 broadcast_in_dim.8
  197.9 0.1 div.35
  198.0 0.0 copy-start.2
  198.0 51.9 %all-gather.3.cloned.1.call-done = bf16[512,2304]{0,1:T(8,128)(2,1)} async-done(((bf16[512,144]{0,1:T(8,128)(2,1)}), bf16[512,2304]{0,1:T(8,128)(2,1)}) %all-gather.3.cloned.1.call-update) | async-done | bytes 2359312 | tf_op jit(solution)/shard_map/all_gather | solution.py:32
  249.8 4.0 %fusion.3 = bf16[512,576]{0,1:T(8,128)(2,1)S(1)} fusion(bf16[2304,576]{0,1:T(8,128)(2,1)} %param.9, bf16[512,2304]{0,1:T(8,128)(2,1)} %all-gather.3.cloned.1.call-done, f32[576]{0:T(1024)S(1)} %div.35), kind=kOutput, calls=%fused_computation.5 | convolution fusion | flops 1360134144 | bytes 5605632 | tf_op jit(solution)/shard_map/dot_general | solution.py:31
  253.8 29.4 %fusion = bf16[512,40]{0,1:T(8,128)(2,1)S(1)} fusion(bf16[512,576]{0,1:T(8,128)(2,1)S(1)} %fusion.3), kind=kCustom, calls=%all-reduce-scatter | all-reduce-scatter fusion | flops 327681 | bytes 631808
  283.3 2.4 collective-permute-start
  285.8 1.3 collective-permute-start.1
  287.1 0.0 copy-done.2
  287.1 0.6 dynamic-slice.4
  288.3 0.0 collective-permute-done.1
  288.3 0.0 collective-permute-done
  288.3 0.3 concatenate
  288.6 0.6 constant_dynamic-slice_fusion
  (2 shorter events, 0.0 us)
Async XLA Ops:
  7.2 25.3 %copy-start = (bf16[576,2304]{1,0:T(8,128)(2,1)S(1)}, bf16[576,2304]{1,0:T(8,128)(2,1)}, u32[]{:S(2)}) copy-start(bf16[576,2304]{1,0:T(8,128)(2,1)} %param.7) | copy-start | bytes 7962628
  7.2 106.0 %reduce-scatter.5.cloned.1.call-start = ((), (), s32[]{:S(2)}) async-start(), calls=%async_computation.2 | async-start | bytes 2506752 | tf_op jit(solution)/shard_map/reduce_scatter | solution.py:23
  32.5 4.8 %copy-start.1 = (bf16[576,512]{1,0:T(8,128)(2,1)S(1)}, bf16[576,512]{1,0:T(8,128)(2,1)}, u32[]{:S(2)}) copy-start(bf16[576,512]{1,0:T(8,128)(2,1)} %reshape.15) | copy-start | bytes 1769476
  37.2 158.8 %reduce-scatter.7.cloned.1.call-start = ((), (), s32[]{:S(2)}) async-start(), calls=%async_computation.3 | async-start | bytes 2506752 | tf_op jit(solution)/shard_map/reduce_scatter | solution.py:26
  42.7 155.1 %copy-start.3 = (s32[1,9]{1,0:T(1,128)S(1)}, s32[1,9]{1,0:T(1,128)}, u32[]{:S(2)}) copy-start(s32[1,9]{1,0:T(1,128)} %param.11) | copy-start | bytes 112
  42.7 207.1 %all-gather.3.cloned.1.call-start = ((), (), s32[]{:S(2)}) async-start(), calls=%async_computation.4 | async-start | bytes 2506752 | tf_op jit(solution)/shard_map/all_gather | solution.py:32
  198.0 89.1 %copy-start.2 = (u32[256]{0:T(256)S(1)}, u32[256]{0:T(256)}, u32[]{:S(2)}) copy-start(u32[256]{0:T(256)} %constant.15) | copy-start | bytes 3076
  283.3 5.0 %collective-permute-start = (bf16[512,40]{0,1:T(8,128)(2,1)S(1)}, bf16[512,40]{0,1:T(8,128)(2,1)S(1)}, u32[]{:S(2)}, u32[]{:S(2)}) collective-permute-start(bf16[512,40]{0,1:T(8,128)(2,1)S(1)} %fusion), channel_id=1, source_target_pairs={{0,1},{1,2},{2,3},{3,4},{4,5},{5,6},{6,7},{7,8},{8,9},{9,10},{10,1... | collective-permute-start | bytes 122888
  285.8 2.5 collective-permute-start.1
Sparse Core Ops, SparseCore 0:
  37.4 75.7 reduce-scatter.4
  116.8 79.2 reduce-scatter.6
  199.1 50.7 all-gather.2
where the time goes:
time: 298 us; the launch traced here: 296 us
  waiting for transfers between devices  205 us (69%)
  blocking collectives  52.9 us (18%)
  between operations  14.5 us (5%)
  matrix products  14.1 us (5%)
  starting transfers between devices  3.85 us (1%)
    reduce_scatter x1, waiting for transfers between devices, on_device(): lax.psum_scatter(up_term.astype(jnp.bfloat16), 'gx', scatter_dimension=1,...  82.9 us
    reduce_scatter x1, waiting for transfers between devices, on_device(): lax.psum_scatter(gate_term.astype(jnp.bfloat16), 'gx', scatter_dimension=...  70.4 us
    all_gather x1, waiting for transfers between devices, on_device(): lax.all_gather(hidden, 'gx', axis=1, tiled=True)  51.9 us
    unnamed x1, blocking collectives  29.4 us
    all_gather x1, blocking collectives, on_device(): piece = lax.all_gather(tokens, 'yz', axis=1, tiled=True)  23.5 us
  transfers between devices with their start and end apart: 5, of which 3 were waited for; matrix products, arithmetic and copies ran while one was open for 2% of the time, Pallas kernels for 0%

commit v1 on v0

v1 whole, which is shorter than its diff:
```python
import functools

import jax
import jax.numpy as jnp
from jax import lax
from jax.experimental import pallas as pl
from jax.experimental.pallas import tpu as pltpu
from jax.sharding import PartitionSpec as P

saturation = 127.0
MESH = pl.DeviceIdType.MESH
f32 = jnp.float32
bf16 = jnp.bfloat16

ROWS = 512
K = 4
L = ROWS // K
FEAT = 576
HID = 2304
BLK = 144
OWN = 36
PAD = 48
QB = 64
NSEM = 64


def kernel(
    t_ref, gw_hbm, uw_hbm, dw_hbm, eh_ref, eo_ref,
    mixed_ref, hidden_ref,
    w_in, w_t, dw, tok, tok_f, tok_b,
    parts, r1a, r1b, s1, r2, hid,
    out_f, ob, obr, oz, ozr,
    local_sem, send_sem, recv_sem,
):
    gx = lax.axis_index("gx")
    yz = lax.axis_index("yz")
    x = lax.rem(gx, 4)
    y = lax.div(gx, 4)
    z = lax.div(yz, 2)
    c = lax.rem(yz, 2)
    gx_at = lambda yy, xx: (yy * 4 + xx, yz)
    at_x = lambda d: gx_at(y, lax.rem(x + d, 4))
    at_y = lambda d: gx_at(lax.rem(y + d, 4), x)
    at_z = lambda d: (gx, lax.rem(z + d, 8) * 2 + c)
    sibling = (gx, z * 2 + 1 - c)

    loads = [
        pltpu.make_async_copy(gw_hbm, w_in.at[0], local_sem.at[0]),
        pltpu.make_async_copy(uw_hbm, w_in.at[1], local_sem.at[1]),
        pltpu.make_async_copy(dw_hbm, dw, local_sem.at[2]),
    ]
    for load in loads:
        load.start()

    barrier = pltpu.get_barrier_semaphore()
    partners = [at_z(d) for d in range(1, 8)] + [sibling]
    partners += [at_x(d) for d in range(1, 4)] + [at_y(d) for d in range(1, 4)]
    for partner in partners:
        pl.semaphore_signal(barrier, inc=1, device_id=partner, device_id_type=MESH)

    for k in range(K):
        tok[k, c, z] = jnp.zeros((PAD, L), bf16)
        tok[k, c, z, 0:OWN, :] = t_ref[:, k * L:(k + 1) * L]
    pl.semaphore_wait(barrier, len(partners))

    sent = {}

    def send(k, i, src, dst, to):
        copy = pltpu.make_async_remote_copy(
            src_ref=src, dst_ref=dst, send_sem=send_sem.at[k, i], recv_sem=recv_sem.at[k, i],
            device_id=to, device_id_type=MESH,
        )
        copy.start()
        sent[k, i] = copy

    def arrived(k, i):
        sent[k, i].wait_recv()

    TOK, TOKC, R1A, R1B, R2, A1, A2, A2F, OC, OZ = 0, 7, 8, 12, 20, 26, 32, 40, 44, 45

    for k in range(K):
        for d in range(1, 8):
            send(k, TOK + d - 1, tok.at[k, c, z], tok.at[k, c, z], at_z(d))

    for m in range(2):
        loads[m].wait()

        @pl.loop(0, HID // 128)
        def _(j):
            cols = pl.ds(pl.multiple_of(j * 128, 128), 128)
            w_t[m, cols, :] = w_in[m, :, cols].T

    place = ((x, y), (y, x))
    first = (at_x, at_y)
    second = (at_y, at_x)

    def piece(k, m, dest, half):
        two = pl.ds(2 * half, 2)
        return parts.at[k, 0, two, dest] if m == 0 else parts.at[k, 1, dest, two]

    def tokens_stage(k):
        for d in range(1, 8):
            arrived(k, TOK + d - 1)
        send(k, TOKC, tok.at[k, c], tok.at[k, c], sibling)

    def first_stage(k):
        arrived(k, TOKC)
        for b in range(16):
            tok_f[b * OWN:(b + 1) * OWN, :] = tok[k, b % 2, b // 2, 0:OWN, :].astype(f32)
        tok_b[...] = tok_f[...].astype(bf16)

        for m in range(2):
            @pl.loop(0, 4)
            def _(j):
                rows = pl.ds(pl.multiple_of(j * FEAT, FEAT), FEAT)
                part = jnp.dot(w_t[m, rows, :], tok_b[...], preferred_element_type=f32)
                terms = []
                for b in range(FEAT // QB):
                    e = eh_ref[0, j * (FEAT // QB) + b]
                    most = jnp.left_shift(jnp.int32(1), e + 16).astype(f32) * (saturation * 2.0 ** -16)
                    terms.append(jnp.clip(part[b * QB:(b + 1) * QB], -most, most).astype(bf16))
                term = jnp.concatenate(terms, axis=0)
                parts[k, m, j] = term.reshape(4, BLK, L)

            p = place[m][0]
            right, left, opposite = lax.rem(p + 1, 4), lax.rem(p + 3, 4), lax.rem(p + 2, 4)
            send(k, R1A + 2 * m, piece(k, m, opposite, 0), r1a.at[k, m, 0], first[m](1))
            send(k, R1A + 2 * m + 1, piece(k, m, opposite, 1), r1a.at[k, m, 1], first[m](3))
            send(k, R1B + 4 * m, piece(k, m, right, 1), r1b.at[k, m, 0, 1], first[m](1))
            send(k, R1B + 4 * m + 1, piece(k, m, left, 0), r1b.at[k, m, 1, 0], first[m](3))

    def second_stage(k):
        for m in range(2):
            p = place[m][0]
            right, left = lax.rem(p + 1, 4), lax.rem(p + 3, 4)
            for half, dest, way in ((0, right, 1), (1, left, 3)):
                arrived(k, R1A + 2 * m + half)
                mine = piece(k, m, dest, half)
                mine[...] = (mine[...].astype(f32) + r1a[k, m, half].astype(f32)).astype(bf16)
                send(k, R1B + 4 * m + 2 + half, mine, r1b.at[k, m, half, half], first[m](way))

    def third_stage(k):
        for m in range(2):
            p, q = place[m]
            for i in range(4):
                arrived(k, R1B + 4 * m + i)
            for half in range(2):
                total = piece(k, m, p, half)[...].astype(f32)
                total += r1b[k, m, 0, half].astype(f32)
                total += r1b[k, m, 1, half].astype(f32)
                s1[k, m, 2 * half:2 * half + 2] = total.astype(bf16)
            for d in range(1, 4):
                send(k, R2 + 3 * m + d - 1, s1.at[k, m, lax.rem(q + d, 4)], r2.at[k, m, d - 1], second[m](d))

    def cut(k):
        low = 80 if k % 2 == 0 else 64
        return (pl.ds(0, low), pl.ds(low, BLK - low))

    def fourth_stage(k):
        sums = []
        for m in range(2):
            q = place[m][1]
            total = s1[k, m, q].astype(f32)
            for d in range(1, 4):
                arrived(k, R2 + 3 * m + d - 1)
                total += r2[k, m, d - 1].astype(f32)
            sums.append(total)
        gate_sum, up_sum = sums
        hidden = (gate_sum / (1.0 + jnp.exp(-gate_sum)) * up_sum).astype(bf16)
        hid[k, y, x] = hidden
        hidden_ref[:, k * L:(k + 1) * L] = hidden
        for h in range(2):
            own = hid.at[k, y, x, cut(k)[h]]
            for d in range(1, 4):
                send(k, A1 + 3 * h + d - 1, own, own, first[h](d))

    def line(k, h, at, half):
        two = pl.ds(2 * half, 2)
        return hid.at[k, at, two, cut(k)[h]] if h == 0 else hid.at[k, two, at, cut(k)[h]]

    def fifth_stage(k):
        for h in range(2):
            for d in range(1, 4):
                arrived(k, A1 + 3 * h + d - 1)
            q = place[h][1]
            for i, (half, way) in enumerate(((0, 1), (1, 3), (1, 1), (0, 3))):
                ref = line(k, h, q, half)
                send(k, A2 + 4 * h + i, ref, ref, second[h](way))

    def sixth_stage(k):
        for h in range(2):
            q = place[h][1]
            for half, way in ((0, 1), (1, 3)):
                arrived(k, A2 + 4 * h + half)
                ref = line(k, h, lax.rem(q + (3 if half == 0 else 1), 4), half)
                send(k, A2F + 2 * h + half, ref, ref, second[h](way))

    def seventh_stage(k):
        for h in range(2):
            arrived(k, A2 + 4 * h + 2)
            arrived(k, A2 + 4 * h + 3)
            arrived(k, A2F + 2 * h)
            arrived(k, A2F + 2 * h + 1)
        whole = hid[k].reshape(HID, L)

        @pl.loop(0, 3)
        def _(j):
            rows = pl.ds(pl.multiple_of(j * 192, 192), 192)
            part = jnp.dot(dw[rows, :], whole, preferred_element_type=f32)
            for b in range(3):
                e = eo_ref[0, j * 3 + b]
                most = jnp.left_shift(jnp.int32(1), e + 16).astype(f32) * (saturation * 2.0 ** -16)
                out_f[pl.ds(pl.multiple_of(j * 192 + b * QB, QB), QB), :] = jnp.clip(part[b * QB:(b + 1) * QB], -most, most)

        for b in range(16):
            ob[k, b % 2, b // 2, 0:OWN, :] = out_f[b * OWN:(b + 1) * OWN, :].astype(bf16)
        send(k, OC, ob.at[k, 1 - c], obr.at[k], sibling)

    def eighth_stage(k):
        arrived(k, OC)
        oz[k] = (ob[k, c].astype(f32) + obr[k].astype(f32)).astype(bf16)
        for d in range(1, 8):
            send(k, OZ + d - 1, oz.at[k, lax.rem(z + d, 8)], ozr.at[k, d - 1], at_z(d))

    def last_stage(k):
        total = oz[k, z].astype(f32)
        for d in range(1, 8):
            arrived(k, OZ + d - 1)
            total += ozr[k, d - 1].astype(f32)
        mixed_ref[:, k * L:(k + 1) * L] = total[0:OWN].astype(bf16)

    for k in range(K):
        for b in range(2):
            ob[k, b] = jnp.zeros((8, PAD, L), bf16)

    stages = (
        tokens_stage, first_stage, second_stage, third_stage, fourth_stage, fifth_stage,
        sixth_stage, seventh_stage, eighth_stage, last_stage,
    )
    for slot in range(len(stages) + K - 1):
        if slot == K:
            loads[2].wait()
        for k in range(K):
            s = slot - k
            if 0 <= s < len(stages):
                stages[s](k)

    for copy in sent.values():
        copy.wait_send()


def on_device(tokens, gate_weight, up_weight, down_weight, exponents_hidden, exponents_output):
    vmem = pl.BlockSpec(memory_space=pltpu.VMEM)
    smem = pl.BlockSpec(memory_space=pltpu.SMEM)
    hbm = pl.BlockSpec(memory_space=pl.ANY)
    mixed, hidden = pl.pallas_call(
        kernel,
        out_shape=(
            jax.ShapeDtypeStruct((OWN, ROWS), bf16),
            jax.ShapeDtypeStruct((BLK, ROWS), bf16),
        ),
        in_specs=[vmem, hbm, hbm, hbm, smem, smem],
        out_specs=(vmem, vmem),
        scratch_shapes=[
            pltpu.VMEM((2, FEAT, HID), bf16),
            pltpu.VMEM((2, HID, FEAT), bf16),
            pltpu.VMEM((FEAT, HID), bf16),
            pltpu.VMEM((K, 2, 8, PAD, L), bf16),
            pltpu.VMEM((FEAT, L), f32),
            pltpu.VMEM((FEAT, L), bf16),
            pltpu.VMEM((K, 2, 4, 4, BLK, L), bf16),
            pltpu.VMEM((K, 2, 2, 2, BLK, L), bf16),
            pltpu.VMEM((K, 2, 2, 2, 2, BLK, L), bf16),
            pltpu.VMEM((K, 2, 4, BLK, L), bf16),
            pltpu.VMEM((K, 2, 3, BLK, L), bf16),
            pltpu.VMEM((K, 4, 4, BLK, L), bf16),
            pltpu.VMEM((FEAT, L), f32),
            pltpu.VMEM((K, 2, 8, PAD, L), bf16),
            pltpu.VMEM((K, 8, PAD, L), bf16),
            pltpu.VMEM((K, 8, PAD, L), bf16),
            pltpu.VMEM((K, 7, PAD, L), bf16),
            pltpu.SemaphoreType.DMA((3,)),
            pltpu.SemaphoreType.DMA((K, NSEM)),
            pltpu.SemaphoreType.DMA((K, NSEM)),
        ],
        compiler_params=pltpu.CompilerParams(
            collective_id=0, has_side_effects=True, vmem_limit_bytes=56 << 20
        ),
    )(tokens.T, gate_weight, up_weight, down_weight.T, exponents_hidden, exponents_output)
    return mixed.T, hidden.T


def solution(mesh):
    placed = (
        P(None, ("gx", "yz")),
        P("gx", "yz"),
        P("gx", "yz"),
        P("yz", "gx"),
        P("gx", "yz"),
        P("yz", "gx"),
    )
    return jax.shard_map(
        on_device,
        mesh=mesh,
        in_specs=placed,
        out_specs=(P(None, ("gx", "yz")), P(None, ("yz", "gx"))),
        check_vma=False,
    )
```

time: 298 us -> 88.3 us (0.30)
  waiting for transfers between devices: 205 us -> 0 us
  Pallas kernels: 0 us -> 83.3 us
  blocking collectives: 52.9 us -> 0 us
  matrix products: 14.1 us -> 0 us
  between operations: 14.5 us -> 0.64 us
  starting transfers between devices: 3.85 us -> 0 us
    reduce_scatter x2 -> x0, waiting for transfers between devices: 153 us -> none  [the longest x1 82.9 us: on_device(): lax.psum_scatter(up_term.astype(jnp.bfloat16), 'gx', scatter_dimension=1,...]
    pallas_call x0 -> x1, Pallas kernels: none -> 83.3 us  [on_device(): pl.pallas_call(kernel, out_shape=(jax.ShapeDtypeStruct((OWN, ROWS), bf16)...]
    all_gather x1 -> x0, waiting for transfers between devices: 51.9 us -> none  [on_device(): lax.all_gather(hidden, 'gx', axis=1, tiled=True)]
    unnamed x1 -> x0, blocking collectives: 29.4 us -> none
    all_gather x1 -> x0, blocking collectives: 23.5 us -> none  [on_device(): piece = lax.all_gather(tokens, 'yz', axis=1, tiled=True)]
    dot_general x3 -> x0, matrix products: 14.1 us -> none  [the longest x1 5.37 us: on_device(): up_part = jnp.dot(piece, up_weight, preferred_element_type=jnp.float32)]
    unnamed x2 -> x0, starting transfers between devices: 3.73 us -> none
  transfers between devices with their start and end apart: 5 -> 0, of which waited for: 3 -> 0; matrix products, arithmetic and copies ran while one was open for 2% -> 0% of each run, Pallas kernels for 0% -> 0%
where the time goes in v1:
time: 88.3 us; the launch traced here: 86.9 us
  Pallas kernels  83.3 us (94%)
  local copies, waits for them, and re-layouts  2.98 us (3%)
    pallas_call x1, Pallas kernels, on_device(): pl.pallas_call(kernel, out_shape=(jax.ShapeDtypeStruct((OWN, ROWS), bf16)...  83.3 us
    unnamed x2, local copies, waits for them, and re-layouts  2.98 us

profile of v1, /device:TPU:1, one launch (start us, length us, event | category | flops | bytes accessed | tf_op | source)
XLA Modules:
  0.0 86.9 jit_solution(7138288256984803603)
XLA Ops:
  0.6 83.3 %shard_map.77 = (bf16[36,512]{1,0:T(8,128)(2,1)}, bf16[144,512]{1,0:T(8,128)(2,1)}) custom-call(bf16[36,512]{1,0:T(8,128)(2,1)} %bitcast.6, bf16[576,2304]{1,0:T(8,128)(2,1)} %gw_hbm.1, bf16[576,2304]{1,0:T(8,128)(2,1)} %uw_hbm.1, bf16[576,2304]{1,0:T(8,128)(2,1)} %bitcast.4, s32[1,36]{1,0:T(1,128)} %eh_ref.1, s32[1,9]{1,0:T(1,128)} %eo_ref.1), custom_call_target="tpu_custom_call" | custom-call | tf_op jit(solution)/shard_map/pallas_call | solution.py:256
  84.0 1.4 %copy.10 = bf16[512,36]{0,1:T(8,128)(2,1)} copy(bf16[512,36]{0,1:T(8,128)(2,1)} %bitcast.7) | data formatting | bytes 73728
  85.3 1.6 %copy.11 = bf16[512,144]{0,1:T(8,128)(2,1)} copy(bf16[512,144]{0,1:T(8,128)(2,1)} %bitcast.5) | data formatting | bytes 294912

commit v2 on v1

v2 whole, which is shorter than its diff:
```python
import functools

import jax
import jax.numpy as jnp
from jax import lax
from jax.experimental import pallas as pl
from jax.experimental.pallas import tpu as pltpu
from jax.sharding import PartitionSpec as P

saturation = 127.0
MESH = pl.DeviceIdType.MESH
f32 = jnp.float32
bf16 = jnp.bfloat16

ROWS = 512
K = 4
L = ROWS // K
FEAT = 576
HID = 2304
BLK = 144
OWN = 36
PAD = 48
QB = 64
NSEM = 64
ORDER = (
    ("TK", 0), ("T", 0), ("Mg", 0), ("Mu", 0), ("TK", 1), ("TK", 2), ("T", 1), ("Ag", 0),
    ("Mu", 1), ("Mg", 1), ("T", 2), ("Au", 0), ("TK", 3), ("Bg", 0), ("Mg", 2), ("Mu", 2),
    ("Bu", 0), ("T", 3), ("Au", 1), ("Mu", 3), ("Ag", 1), ("Mg", 3), ("Ag", 2), ("Bu", 1),
    ("Au", 2), ("Bg", 1), ("Au", 3), ("Ag", 3), ("C", 0), ("Bu", 2), ("Bg", 2), ("C", 1),
    ("Bg", 3), ("Bu", 3), ("D0", 0), ("D1", 0), ("C", 2), ("D1", 1), ("D0", 1), ("C", 3),
    ("E0", 0), ("E1", 0), ("E1", 1), ("D1", 2), ("E0", 1), ("D0", 2), ("D0", 3), ("D1", 3),
    ("F", 0), ("E1", 2), ("E0", 2), ("F", 1), ("E0", 3), ("G", 0), ("E1", 3), ("G", 1),
    ("F", 2), ("G", 2), ("F", 3), ("G", 3), ("H", 2), ("H", 0), ("H", 1), ("H", 3),
)
FAR_FIRST = (4, 3, 5, 2, 6, 1, 7)


def bound(exponent):
    return jnp.left_shift(jnp.int32(1), exponent + 16).astype(f32) * (saturation * 2.0 ** -16)


def kernel(
    t_hbm, gw_hbm, uw_hbm, dw_hbm, eh_ref, eo_ref,
    mixed_ref, hidden_ref,
    t_ref, most, w_in, w_t, dw, tok, tok_f, tok_b,
    parts, r1a, r1b, s1, r2, hid,
    out_f, ob, obr, oz, ozr,
    local_sem, send_sem, recv_sem,
):
    gx = lax.axis_index("gx")
    yz = lax.axis_index("yz")
    x = lax.rem(gx, 4)
    y = lax.div(gx, 4)
    z = lax.div(yz, 2)
    c = lax.rem(yz, 2)
    gx_at = lambda yy, xx: (yy * 4 + xx, yz)
    at_x = lambda d: gx_at(y, lax.rem(x + d, 4))
    at_y = lambda d: gx_at(lax.rem(y + d, 4), x)
    at_z = lambda d: (gx, lax.rem(z + d, 8) * 2 + c)
    sibling = (gx, z * 2 + 1 - c)

    load_t = pltpu.make_async_copy(t_hbm, t_ref, local_sem.at[3])
    load_t.start()
    loads = [
        pltpu.make_async_copy(gw_hbm, w_in.at[0], local_sem.at[0]),
        pltpu.make_async_copy(uw_hbm, w_in.at[1], local_sem.at[1]),
        pltpu.make_async_copy(dw_hbm, dw, local_sem.at[2]),
    ]
    for load in loads:
        load.start()

    barrier = pltpu.get_barrier_semaphore()
    partners = [at_z(d) for d in range(1, 8)] + [sibling]
    partners += [at_x(d) for d in range(1, 4)] + [at_y(d) for d in range(1, 4)]
    for partner in partners:
        pl.semaphore_signal(barrier, inc=1, device_id=partner, device_id_type=MESH)

    load_t.wait()
    for k in range(K):
        tok[k, c, z] = jnp.zeros((PAD, L), bf16)
        tok[k, c, z, 0:OWN, :] = t_ref[:, k * L:(k + 1) * L]
    pl.semaphore_wait(barrier, len(partners))

    sent = {}

    def send(k, i, src, dst, to):
        copy = pltpu.make_async_remote_copy(
            src_ref=src, dst_ref=dst, send_sem=send_sem.at[k, i], recv_sem=recv_sem.at[k, i],
            device_id=to, device_id_type=MESH,
        )
        copy.start()
        sent[k, i] = copy

    def arrived(k, i):
        sent[k, i].wait_recv()

    TOK, TOKC, R1A, R1B, R2, A1, A2, A2F, OC, OZ = 0, 7, 8, 12, 20, 26, 32, 40, 44, 45

    for k in range(K):
        for d in FAR_FIRST:
            send(k, TOK + d - 1, tok.at[k, c, z], tok.at[k, c, z], at_z(d))

    for b in range(HID // QB):
        most[b * QB:(b + 1) * QB, :] = jnp.full((QB, L), bound(eh_ref[0, b])).astype(bf16)

    for m in range(2):
        loads[m].wait()

        @pl.loop(0, HID // 128)
        def _(j):
            cols = pl.ds(pl.multiple_of(j * 128, 128), 128)
            w_t[m, cols, :] = w_in[m, :, cols].T

    place = ((x, y), (y, x))
    first = (at_x, at_y)
    second = (at_y, at_x)

    def piece(k, m, dest, half):
        two = pl.ds(2 * half, 2)
        return parts.at[k, 0, two, dest] if m == 0 else parts.at[k, 1, dest, two]

    def tokens_stage(k):
        for d in range(1, 8):
            arrived(k, TOK + d - 1)
        send(k, TOKC, tok.at[k, c], tok.at[k, c], sibling)

    def assemble(k):
        arrived(k, TOKC)
        for b in range(16):
            tok_f[b * OWN:(b + 1) * OWN, :] = tok[k, b % 2, b // 2, 0:OWN, :].astype(f32)
        tok_b[k] = tok_f[...].astype(bf16)

    def multiply(k, m):
        p = place[m][0]
        for d in (2, 1, 3, 0):
            dest = lax.rem(p + d, 4)
            blocks = [4 * i + dest if m == 0 else 4 * dest + i for i in range(4)]
            rows = [pl.ds(pl.multiple_of(b * BLK, BLK), BLK) for b in blocks]
            weight = jnp.concatenate([w_t[m, r, :] for r in rows], axis=0)
            part = jnp.dot(weight, tok_b[k], preferred_element_type=f32).astype(bf16)
            for i, r in enumerate(rows):
                term = jnp.clip(part[i * BLK:(i + 1) * BLK], -most[r, :], most[r, :])
                if m == 0:
                    parts[k, 0, i, dest] = term
                else:
                    parts[k, 1, dest, i] = term
            if d == 2:
                send(k, R1A + 2 * m, piece(k, m, dest, 0), r1a.at[k, m, 0], first[m](1))
                send(k, R1A + 2 * m + 1, piece(k, m, dest, 1), r1a.at[k, m, 1], first[m](3))
            elif d == 1:
                send(k, R1B + 4 * m, piece(k, m, dest, 1), r1b.at[k, m, 0, 1], first[m](1))
            elif d == 3:
                send(k, R1B + 4 * m + 1, piece(k, m, dest, 0), r1b.at[k, m, 1, 0], first[m](3))

    def middle(k, m):
        p = place[m][0]
        right, left = lax.rem(p + 1, 4), lax.rem(p + 3, 4)
        for half, dest, way in ((0, right, 1), (1, left, 3)):
            arrived(k, R1A + 2 * m + half)
            mine = piece(k, m, dest, half)
            mine[...] = (mine[...].astype(f32) + r1a[k, m, half].astype(f32)).astype(bf16)
            send(k, R1B + 4 * m + 2 + half, mine, r1b.at[k, m, half, half], first[m](way))

    def line_sum(k, m):
        p, q = place[m]
        for i in range(4):
            arrived(k, R1B + 4 * m + i)
        for half in range(2):
            total = piece(k, m, p, half)[...].astype(f32)
            total += r1b[k, m, 0, half].astype(f32)
            total += r1b[k, m, 1, half].astype(f32)
            s1[k, m, 2 * half:2 * half + 2] = total.astype(bf16)
        for d in range(1, 4):
            send(k, R2 + 3 * m + d - 1, s1.at[k, m, lax.rem(q + d, 4)], r2.at[k, m, d - 1], second[m](d))

    def cut(k):
        low = 80 if k % 2 == 0 else 64
        return (pl.ds(0, low), pl.ds(low, BLK - low))

    def gated(k):
        sums = []
        for m in range(2):
            q = place[m][1]
            total = s1[k, m, q].astype(f32)
            for d in range(1, 4):
                arrived(k, R2 + 3 * m + d - 1)
                total += r2[k, m, d - 1].astype(f32)
            sums.append(total)
        gate_sum, up_sum = sums
        hidden = (gate_sum / (1.0 + jnp.exp(-gate_sum)) * up_sum).astype(bf16)
        hid[k, y, x] = hidden
        hidden_ref[:, k * L:(k + 1) * L] = hidden
        for h in range(2):
            own = hid.at[k, y, x, cut(k)[h]]
            for d in range(1, 4):
                send(k, A1 + 3 * h + d - 1, own, own, first[h](d))

    def line(k, h, at, half):
        two = pl.ds(2 * half, 2)
        return hid.at[k, at, two, cut(k)[h]] if h == 0 else hid.at[k, two, at, cut(k)[h]]

    def spread(k, h):
        for d in range(1, 4):
            arrived(k, A1 + 3 * h + d - 1)
        q = place[h][1]
        for i, (half, way) in enumerate(((0, 1), (1, 3), (1, 1), (0, 3))):
            ref = line(k, h, q, half)
            send(k, A2 + 4 * h + i, ref, ref, second[h](way))

    def forward(k, h):
        q = place[h][1]
        for half, way in ((0, 1), (1, 3)):
            arrived(k, A2 + 4 * h + half)
            ref = line(k, h, lax.rem(q + (3 if half == 0 else 1), 4), half)
            send(k, A2F + 2 * h + half, ref, ref, second[h](way))

    def project(k):
        for h in range(2):
            arrived(k, A2 + 4 * h + 2)
            arrived(k, A2 + 4 * h + 3)
            arrived(k, A2F + 2 * h)
            arrived(k, A2F + 2 * h + 1)
        whole = hid[k].reshape(HID, L)

        @pl.loop(0, 3, unroll=3)
        def _(j):
            rows = pl.ds(pl.multiple_of(j * 192, 192), 192)
            part = jnp.dot(dw[rows, :], whole, preferred_element_type=f32)
            for b in range(3):
                limit = bound(eo_ref[0, j * 3 + b])
                out_f[pl.ds(pl.multiple_of(j * 192 + b * QB, QB), QB), :] = jnp.clip(part[b * QB:(b + 1) * QB], -limit, limit)

        for b in range(16):
            ob[k, b % 2, b // 2, 0:OWN, :] = out_f[b * OWN:(b + 1) * OWN, :].astype(bf16)
        send(k, OC, ob.at[k, 1 - c], obr.at[k], sibling)

    def pair_sum(k):
        arrived(k, OC)
        oz[k] = (ob[k, c].astype(f32) + obr[k].astype(f32)).astype(bf16)
        for d in FAR_FIRST:
            send(k, OZ + d - 1, oz.at[k, lax.rem(z + d, 8)], ozr.at[k, d - 1], at_z(d))

    def finish(k):
        total = oz[k, z].astype(f32)
        for d in range(1, 8):
            arrived(k, OZ + d - 1)
            total += ozr[k, d - 1].astype(f32)
        mixed_ref[:, k * L:(k + 1) * L] = total[0:OWN].astype(bf16)

    for k in range(K):
        for b in range(2):
            ob[k, b] = jnp.zeros((8, PAD, L), bf16)

    stages = {
        "TK": tokens_stage, "T": assemble,
        "Mg": lambda k: multiply(k, 0), "Mu": lambda k: multiply(k, 1),
        "Ag": lambda k: middle(k, 0), "Au": lambda k: middle(k, 1),
        "Bg": lambda k: line_sum(k, 0), "Bu": lambda k: line_sum(k, 1),
        "C": gated,
        "D0": lambda k: spread(k, 0), "D1": lambda k: spread(k, 1),
        "E0": lambda k: forward(k, 0), "E1": lambda k: forward(k, 1),
        "F": project, "G": pair_sum, "H": finish,
    }
    for stage, k in ORDER:
        if (stage, k) == ("F", 0):
            loads[2].wait()
        stages[stage](k)

    for copy in sent.values():
        copy.wait_send()


def on_device(tokens, gate_weight, up_weight, down_weight, exponents_hidden, exponents_output):
    smem = pl.BlockSpec(memory_space=pltpu.SMEM)
    hbm = pl.BlockSpec(memory_space=pl.ANY)
    mixed, hidden = pl.pallas_call(
        kernel,
        out_shape=(
            pltpu.VMEM((OWN, ROWS), bf16),
            pltpu.VMEM((BLK, ROWS), bf16),
        ),
        in_specs=[hbm, hbm, hbm, hbm, smem, smem],
        out_specs=(pl.BlockSpec(memory_space=pltpu.VMEM), pl.BlockSpec(memory_space=pltpu.VMEM)),
        scratch_shapes=[
            pltpu.VMEM((OWN, ROWS), bf16),
            pltpu.VMEM((HID, L), bf16),
            pltpu.VMEM((2, FEAT, HID), bf16),
            pltpu.VMEM((2, HID, FEAT), bf16),
            pltpu.VMEM((FEAT, HID), bf16),
            pltpu.VMEM((K, 2, 8, PAD, L), bf16),
            pltpu.VMEM((FEAT, L), f32),
            pltpu.VMEM((K, FEAT, L), bf16),
            pltpu.VMEM((K, 2, 4, 4, BLK, L), bf16),
            pltpu.VMEM((K, 2, 2, 2, BLK, L), bf16),
            pltpu.VMEM((K, 2, 2, 2, 2, BLK, L), bf16),
            pltpu.VMEM((K, 2, 4, BLK, L), bf16),
            pltpu.VMEM((K, 2, 3, BLK, L), bf16),
            pltpu.VMEM((K, 4, 4, BLK, L), bf16),
            pltpu.VMEM((FEAT, L), f32),
            pltpu.VMEM((K, 2, 8, PAD, L), bf16),
            pltpu.VMEM((K, 8, PAD, L), bf16),
            pltpu.VMEM((K, 8, PAD, L), bf16),
            pltpu.VMEM((K, 7, PAD, L), bf16),
            pltpu.SemaphoreType.DMA((4,)),
            pltpu.SemaphoreType.DMA((K, NSEM)),
            pltpu.SemaphoreType.DMA((K, NSEM)),
        ],
        compiler_params=pltpu.CompilerParams(
            collective_id=0, has_side_effects=True, vmem_limit_bytes=56 << 20
        ),
    )(tokens.T, gate_weight, up_weight, down_weight.T, exponents_hidden, exponents_output)
    return mixed.T, hidden.T


def solution(mesh):
    placed = (
        P(None, ("gx", "yz")),
        P("gx", "yz"),
        P("gx", "yz"),
        P("yz", "gx"),
        P("gx", "yz"),
        P("yz", "gx"),
    )
    return jax.shard_map(
        on_device,
        mesh=mesh,
        in_specs=placed,
        out_specs=(P(None, ("gx", "yz")), P(None, ("yz", "gx"))),
        check_vma=False,
    )
```

time: 88.3 us -> 75.6 us (0.86); the launches traced: 86.9 us -> 75.5 us
  Pallas kernels: 83.3 us -> 73.6 us
  local copies, waits for them, and re-layouts: 2.98 us -> 1.28 us
    pallas_call x1, Pallas kernels: 83.3 us -> 73.6 us  [on_device(): pl.pallas_call(kernel, out_shape=(pltpu.VMEM((OWN, ROWS), bf16), pltpu.VM...]
    unnamed x2, local copies, waits for them, and re-layouts: 2.98 us -> 1.28 us
where the time goes in v2:
time: 75.6 us; the launch traced here: 75.5 us
  Pallas kernels  73.6 us (97%)
  local copies, waits for them, and re-layouts  1.28 us (2%)
    pallas_call x1, Pallas kernels, on_device(): pl.pallas_call(kernel, out_shape=(pltpu.VMEM((OWN, ROWS), bf16), pltpu.VM...  73.6 us

profile of v2, /device:TPU:1, one launch (start us, length us, event | category | flops | bytes accessed | tf_op | source)
XLA Modules:
  0.0 75.5 jit_solution(12153623139665885605)
XLA Ops:
  0.6 73.6 %shard_map.77 = (bf16[36,512]{1,0:T(8,128)(2,1)S(1)}, bf16[144,512]{1,0:T(8,128)(2,1)S(1)}) custom-call(bf16[36,512]{1,0:T(8,128)(2,1)} %bitcast.7, bf16[576,2304]{1,0:T(8,128)(2,1)} %gw_hbm.1, bf16[576,2304]{1,0:T(8,128)(2,1)} %uw_hbm.1, bf16[576,2304]{1,0:T(8,128)(2,1)} %bitcast.6, s32[1,36]{1,0:T(1,128)} %eh_ref.1, s32[1,9]{1,0:T(1,128)} %eo_ref.1), custom_call_target="tpu_custom_call" | custom-call | tf_op jit(solution)/shard_map/pallas_call | solution.py:276
  74.3 0.6 copy.10
  74.9 0.7 copy.11

commit v3 on v2

--- a/solution.py
+++ b/solution.py
@@ -261,13 +261,20 @@
         "E0": lambda k: forward(k, 0), "E1": lambda k: forward(k, 1),
         "F": project, "G": pair_sum, "H": finish,
     }
+    settled = set()
     for stage, k in ORDER:
         if (stage, k) == ("F", 0):
             loads[2].wait()
+        if stage == "H":
+            for key, copy in sent.items():
+                if key not in settled and (key[0] < K - 1 or key[1] < OZ):
+                    copy.wait_send()
+                    settled.add(key)
         stages[stage](k)
 
-    for copy in sent.values():
-        copy.wait_send()
+    for key, copy in sent.items():
+        if key not in settled:
+            copy.wait_send()
 
 
 def on_device(tokens, gate_weight, up_weight, down_weight, exponents_hidden, exponents_output):

time: 75.6 us -> 75.3 us (level)
  no operation moved by 1% of the time
where the time goes in v3:
time: 75.3 us; the launch traced here: 75.2 us
  Pallas kernels  73.3 us (97%)
  local copies, waits for them, and re-layouts  1.28 us (2%)
    pallas_call x1, Pallas kernels, on_device(): pl.pallas_call(kernel, out_shape=(pltpu.VMEM((OWN, ROWS), bf16), pltpu.VM...  73.3 us

profile of v3, /device:TPU:1, one launch (start us, length us, event | category | flops | bytes accessed | tf_op | source)
XLA Modules:
  0.0 75.2 jit_solution(10432002680750003829)
XLA Ops:
  0.6 73.3 %shard_map.77 = (bf16[36,512]{1,0:T(8,128)(2,1)S(1)}, bf16[144,512]{1,0:T(8,128)(2,1)S(1)}) custom-call(bf16[36,512]{1,0:T(8,128)(2,1)} %bitcast.7, bf16[576,2304]{1,0:T(8,128)(2,1)} %gw_hbm.1, bf16[576,2304]{1,0:T(8,128)(2,1)} %uw_hbm.1, bf16[576,2304]{1,0:T(8,128)(2,1)} %bitcast.6, s32[1,36]{1,0:T(1,128)} %eh_ref.1, s32[1,9]{1,0:T(1,128)} %eo_ref.1), custom_call_target="tpu_custom_call" | custom-call | tf_op jit(solution)/shard_map/pallas_call | solution.py:283
  74.0 0.6 copy.10
  74.6 0.7 copy.11

commit v4 on v3

--- a/solution.py
+++ b/solution.py
@@ -59,6 +59,12 @@
     at_z = lambda d: (gx, lax.rem(z + d, 8) * 2 + c)
     sibling = (gx, z * 2 + 1 - c)
 
+    barrier = pltpu.get_barrier_semaphore()
+    partners = [at_z(d) for d in range(1, 8)] + [sibling]
+    partners += [at_x(d) for d in range(1, 4)] + [at_y(d) for d in range(1, 4)]
+    for partner in partners:
+        pl.semaphore_signal(barrier, inc=1, device_id=partner, device_id_type=MESH)
+
     load_t = pltpu.make_async_copy(t_hbm, t_ref, local_sem.at[3])
     load_t.start()
     loads = [
@@ -68,12 +74,6 @@
     ]
     for load in loads:
         load.start()
-
-    barrier = pltpu.get_barrier_semaphore()
-    partners = [at_z(d) for d in range(1, 8)] + [sibling]
-    partners += [at_x(d) for d in range(1, 4)] + [at_y(d) for d in range(1, 4)]
-    for partner in partners:
-        pl.semaphore_signal(barrier, inc=1, device_id=partner, device_id_type=MESH)
 
     load_t.wait()
     for k in range(K):
@@ -236,9 +236,11 @@
 
     def pair_sum(k):
         arrived(k, OC)
-        oz[k] = (ob[k, c].astype(f32) + obr[k].astype(f32)).astype(bf16)
-        for d in FAR_FIRST:
-            send(k, OZ + d - 1, oz.at[k, lax.rem(z + d, 8)], ozr.at[k, d - 1], at_z(d))
+        for d in FAR_FIRST + (0,):
+            to = lax.rem(z + d, 8)
+            oz[k, to] = (ob[k, c, to].astype(f32) + obr[k, to].astype(f32)).astype(bf16)
+            if d:
+                send(k, OZ + d - 1, oz.at[k, to], ozr.at[k, d - 1], at_z(d))
 
     def finish(k):
         total = oz[k, z].astype(f32)

time: 75.3 us -> 75.2 us (level)
  no operation moved by 1% of the time
where the time goes in v4:
time: 75.2 us
  Pallas kernels  73.2 us (97%)
  local copies, waits for them, and re-layouts  1.28 us (2%)
    pallas_call x1, Pallas kernels, on_device(): pl.pallas_call(kernel, out_shape=(pltpu.VMEM((OWN, ROWS), bf16), pltpu.VM...  73.2 us

profile of v4, /device:TPU:1, one launch (start us, length us, event | category | flops | bytes accessed | tf_op | source)
XLA Modules:
  0.0 75.2 jit_solution(13075870329513417174)
XLA Ops:
  0.6 73.2 %shard_map.77 = (bf16[36,512]{1,0:T(8,128)(2,1)S(1)}, bf16[144,512]{1,0:T(8,128)(2,1)S(1)}) custom-call(bf16[36,512]{1,0:T(8,128)(2,1)} %bitcast.7, bf16[576,2304]{1,0:T(8,128)(2,1)} %gw_hbm.1, bf16[576,2304]{1,0:T(8,128)(2,1)} %uw_hbm.1, bf16[576,2304]{1,0:T(8,128)(2,1)} %bitcast.6, s32[1,36]{1,0:T(1,128)} %eh_ref.1, s32[1,9]{1,0:T(1,128)} %eo_ref.1), custom_call_target="tpu_custom_call" | custom-call | tf_op jit(solution)/shard_map/pallas_call | solution.py:285
  73.9 0.6 copy.10
  74.5 0.7 copy.11
